TPU v7x, 512 devices: a whole 4x4x16 slice. The times are simulated.
512 devices in a mesh: row: 16 (over z), col: 32 (over x, y, core).
Axes of the slice: x: 4, y: 4, z: 16, core: 2. Of those that a mesh axis runs over, the one named last changes fastest.
Arguments:
- coords: float32 [3, 65536], P(None, ('row', 'col')), may hold values from -1 to 1
- residual_in: float32 [65536, 512], P(('row', 'col')), may hold values from -6 to 6
- link_mask: int32 [512, 2], P(('row', 'col')), may hold values 0 or 1
- compress: float32 [65536, 256], P(('row', 'col')), may hold values from -0.5 to 0.5
- expand: float32 [65536, 256], P(('row', 'col')), may hold values from -0.375 to 0.375
- level_gain: float32 [512, 1280], P(('row', 'col')), may hold values from 0.5 to 1.5
- level_couple: float32 [131072, 1280], P(('row', 'col')), may hold values from -0.1875 to 0.1875
- partner_perm: int32 [512, 5, 256], P(('row', 'col')), may hold values from 0 to 255, each once within a row
Outputs:
- new_residual: float32 [65536, 512], P(('row', 'col'))
- res_norms: float32 [512], replicated
Inputs may be any that keep to these rules, and one draw needn't show every extreme that they name: `partner_perm`: each row of 256 entries names every number once.
All inputs are finite; a program needn't handle non-finite values. No bound on the sum of `link_mask` on one device may be relied on, other than what follows from the above.
Results may differ from a plain program's by a relative error of at most 0.0003.
Values sent between devices are 32-bit elements; how exact they have to be, the bound alone decides.
No kernel may reach another device: no remote copies, remote signals or barrier semaphores. Data moves between devices by JAX's collectives and lax.ppermute only.
A program may use at most 64 MiB of HBM per device.

v0:
```python
import jax
import jax.numpy as jnp
from jax import lax
from jax.sharding import PartitionSpec as P

ROW_LEVELS = 2
COL_LEVELS = 3
WAVENUM = 6.0
SOFTEN = 0.01


def in_blocks(shard, dim, length):
    shape = shard.shape
    tiles = shard.reshape(*shape[:dim], length, shape[dim] // length, *shape[dim + 1 :])
    return jnp.moveaxis(tiles, dim, 0)


def sent_and_summed(shard, axis, dim):
    length = lax.axis_size(axis)
    tiles = lax.all_to_all(in_blocks(shard, dim, length), axis, 0, 0, tiled=True)
    return jnp.sum(tiles, axis=0)


def side_by_side(arrays, axis, dim, along):
    widths = [a.shape[along] for a in arrays]
    both = jnp.concatenate(arrays, axis=along)
    whole = sent_and_summed(both, axis, dim)
    return tuple(jnp.split(whole, [sum(widths[:k]) for k in range(1, len(widths))], axis=along))


def from_everyone(shard, axis):
    length = lax.axis_size(axis)
    return lax.all_to_all(
        jnp.broadcast_to(shard[None], (length, *shard.shape)), axis, 0, 0, tiled=True
    )


def over_copies(shard, axis):
    return from_everyone(shard, axis).sum(axis=0)


def packed_total(arrays, axis):
    ends = [0]
    for a in arrays:
        ends.append(ends[-1] + a.size)
    so_far = over_copies(jnp.concatenate([a.ravel() for a in arrays]), axis)
    return tuple((so_far[b:e].reshape(a.shape) for a, b, e in zip(arrays, ends, ends[1:])))


def gather_turned(arrays, axis, dims):
    turned = [jnp.moveaxis(a, dim, 0) for a, dim in zip(arrays, dims)]
    both = jnp.concatenate([t.reshape(len(t), -1) for t in turned], axis=1)
    whole, at, finished = (lax.all_gather(both, axis, axis=0, tiled=True), 0, [])
    for t, dim in zip(turned, dims):
        piece = whole[:, at : at + t[0].size].reshape(-1, *t.shape[1:])
        finished.append(jnp.moveaxis(piece, 0, dim))
        at += t[0].size
    return tuple(finished)


def from_behind(block, axis, distance):
    devices = range(lax.axis_size(axis))
    route = [(i - distance, i) for i in devices if i - distance in devices]
    return lax.ppermute(block, axis, route)


def from_partner(block, axis, distance):
    count = lax.axis_size(axis)
    route = []
    for low in range(count):
        high = low | 1 << distance
        if high != low and high < count:
            route += [(low, high), (high, low)]
    return lax.ppermute(block, axis, route)


def kernel_tile(own_xyz, other_xyz):
    dist_sq = (own_xyz[0][:, None] - other_xyz[0][None, :]) ** 2
    dist_sq = dist_sq + (own_xyz[1][:, None] - other_xyz[1][None, :]) ** 2
    dist_sq = dist_sq + (own_xyz[2][:, None] - other_xyz[2][None, :]) ** 2
    return jnp.cos(WAVENUM * jnp.sqrt(dist_sq)) / jnp.sqrt(dist_sq + SOFTEN)


def matmul_hi(left, right):
    return jnp.dot(left, right, precision=lax.Precision.HIGHEST)


def inner_cols(left, right):
    return lax.dot_general(left, right, (((0,), (0,)), ((), ())), precision=lax.Precision.HIGHEST)


def chol_solve(gram_mat, cross_mat):
    factor = jnp.linalg.cholesky(gram_mat)
    middle = lax.linalg.triangular_solve(factor, cross_mat, left_side=True, lower=True)
    return lax.linalg.triangular_solve(factor, middle, left_side=True, lower=True, transpose_a=True)


def global_sum(members):
    shares = side_by_side((members[0], members[1], members[2]), "col", 1, 0)
    shares = packed_total((shares[0], shares[1], shares[2]), "row")
    return gather_turned((shares[0], shares[1], shares[2]), "col", (1, 1, 1))


def shards(
    coords, residual_in, link_mask, compress, expand, level_gain, level_couple, partner_perm
):
    below_xyz, below_rhs = from_behind((coords, residual_in), ("row", "col"), 1)
    above_xyz, above_rhs = from_behind((coords, residual_in), ("row", "col"), -1)
    rank_width = compress.shape[1]
    coeffs = inner_cols(compress, residual_in)

    def mix_level(current, partner, level_at):
        taken_rows = partner_perm[0, level_at]
        picked = jnp.take(partner, taken_rows, axis=0)
        gain_col = level_gain[0, level_at * rank_width : (level_at + 1) * rank_width][:, None]
        couple = level_couple[:, level_at * rank_width : (level_at + 1) * rank_width]
        return gain_col * current + matmul_hi(couple, picked)

    row_top = lax.axis_size("row").bit_length() - 2
    for index_row in range(ROW_LEVELS):
        partner = from_partner(coeffs, "row", row_top - index_row)
        coeffs = mix_level(coeffs, partner, index_row)
    col_top = lax.axis_size("col").bit_length() - 2
    for index_col in range(COL_LEVELS):
        partner = from_partner(coeffs, "col", col_top - index_col)
        coeffs = mix_level(coeffs, partner, ROW_LEVELS + index_col)
    far_field = matmul_hi(expand, coeffs)
    weights = link_mask.astype(jnp.float32)
    near_scale = (3.0 * coords.shape[1]) ** (-0.5)
    near_field = matmul_hi(kernel_tile(coords, coords), residual_in)
    near_field = near_field + weights[0, 0] * matmul_hi(kernel_tile(coords, below_xyz), below_rhs)
    near_field = near_field + weights[0, 1] * matmul_hi(kernel_tile(coords, above_xyz), above_rhs)
    near_field = near_scale * near_field
    image = 2.0 * residual_in + near_field + far_field
    gram_mat = inner_cols(image, image)
    cross_mat = inner_cols(image, residual_in)
    points_total = coords.shape[1] * lax.axis_size("row") * lax.axis_size("col")
    self_squares = jnp.sum(residual_in * residual_in, axis=0)[None, :]
    gram_mat, cross_mat, self_total = global_sum((gram_mat, cross_mat, self_squares))
    alpha_mix = chol_solve(gram_mat, cross_mat)
    new_residual = residual_in - matmul_hi(image, alpha_mix)
    col_total = self_total[0] - jnp.sum(alpha_mix * cross_mat, axis=0)
    res_norms = jnp.sqrt(col_total / points_total)
    return (new_residual, res_norms)


def solution(mesh):
    return jax.shard_map(
        shards,
        mesh=mesh,
        in_specs=(
            P(None, ("row", "col")),
            P(("row", "col"), None),
            P(("row", "col"), None),
            P(("row", "col"), None),
            P(("row", "col"), None),
            P(("row", "col"), None),
            P(("row", "col"), None),
            P(("row", "col"), None, None),
        ),
        out_specs=(P(("row", "col"), None), P()),
        check_vma=False,
    )
```

profile of v0, /device:TPU:1, one launch (start us, length us, event | category | flops | bytes accessed | tf_op | source)
XLA Modules:
  0.0 549.9 jit_solution(8922406250387740012)
XLA Ops:
  7.2 4.6 collective-permute-start
  11.8 6.0 %collective-permute-start.2 = (f32[3,128]{1,0:T(4,128)}, f32[3,128]{1,0:T(4,128)}, u32[]{:S(2)}, u32[]{:S(2)}) collective-permute-start(f32[3,128]{1,0:T(4,128)} %param.10), channel_id=1, source_target_pairs={{1,0},{2,1},{3,2},{4,3},{5,4},{6,5},{7,6},{8,7},{9,8},{10,9},{11,1... | collective-permute-start | bytes 4616 | tf_op jit(solution)/shard_map/ppermute | solution.py:64
  17.9 1.9 collective-permute-start.1
  19.8 2.4 collective-permute-start.3
  23.8 16.8 %collective-permute-start.4 = (f32[256,512]{1,0:T(8,128)S(1)}, f32[256,512]{1,0:T(8,128)S(1)}, u32[]{:S(2)}, u32[]{:S(2)}) collective-permute-start(f32[256,512]{1,0:T(8,128)S(1)} %fusion.166), channel_id=1, source_target_pairs={{0,256},{256,0},{32,288},{288,32},{64,320},{320,64},{96,352},{352,... | collective-permute-start | bytes 1572872 | tf_op jit(solution)/shard_map/ppermute | solution.py:74
  45.5 8.0 %collective-permute-done.4 = f32[256,512]{1,0:T(8,128)S(1)} collective-permute-done((f32[256,512]{1,0:T(8,128)S(1)}, f32[256,512]{1,0:T(8,128)S(1)}, u32[]{:S(2)}, u32[]{:S(2)}) %collective-permute-start.4) | collective-permute-done | bytes 524320 | tf_op jit(solution)/shard_map/ppermute | solution.py:74
  56.2 36.6 %collective-permute-start.5 = (f32[256,512]{1,0:T(8,128)S(1)}, f32[256,512]{1,0:T(8,128)S(1)}, u32[]{:S(2)}, u32[]{:S(2)}) collective-permute-start(f32[256,512]{1,0:T(8,128)S(1)} %fusion), channel_id=1, source_target_pairs={{0,128},{128,0},{32,160},{160,32},{64,192},{192,64},{96,224},{224,... | collective-permute-start | bytes 1572872 | tf_op jit(solution)/shard_map/ppermute | solution.py:74
  92.8 42.3 %collective-permute-done.5 = f32[256,512]{1,0:T(8,128)S(1)} collective-permute-done((f32[256,512]{1,0:T(8,128)S(1)}, f32[256,512]{1,0:T(8,128)S(1)}, u32[]{:S(2)}, u32[]{:S(2)}) %collective-permute-start.5) | collective-permute-done | bytes 524320 | tf_op jit(solution)/shard_map/ppermute | solution.py:74
  141.2 13.1 %collective-permute-done.6 = f32[256,512]{1,0:T(8,128)S(1)} collective-permute-done((f32[256,512]{1,0:T(8,128)S(1)}, f32[256,512]{1,0:T(8,128)S(1)}, u32[]{:S(2)}, u32[]{:S(2)}) %collective-permute-start.6) | collective-permute-done | bytes 524320 | tf_op jit(solution)/shard_map/ppermute | solution.py:74
  161.7 9.3 %collective-permute-done.7 = f32[256,512]{1,0:T(8,128)S(1)} collective-permute-done((f32[256,512]{1,0:T(8,128)S(1)}, f32[256,512]{1,0:T(8,128)S(1)}, u32[]{:S(2)}, u32[]{:S(2)}) %collective-permute-start.7) | collective-permute-done | bytes 524320 | tf_op jit(solution)/shard_map/ppermute | solution.py:74
  173.8 2.1 collective-permute-start.8
  179.4 9.0 %collective-permute-done.8 = f32[256,512]{1,0:T(8,128)S(1)} collective-permute-done((f32[256,512]{1,0:T(8,128)S(1)}, f32[256,512]{1,0:T(8,128)S(1)}, u32[]{:S(2)}, u32[]{:S(2)}) %collective-permute-start.8) | collective-permute-done | bytes 524320 | tf_op jit(solution)/shard_map/ppermute | solution.py:74
  194.1 37.4 %all_to_all.11 = f32[32,1025,16]{1,2,0:T(8,128)S(1)} all-to-all(f32[32,1025,16]{1,2,0:T(8,128)S(1)} %maximum_bitcast_fusion), channel_id=1, replica_groups=mesh['row'=16,'col'=32] {'col'}, dimensions={0} | all-to-all | bytes 4198400 | tf_op jit(solution)/shard_map/all_to_all | solution.py:20
  232.9 66.4 %all_to_all.12 = f32[16,1,16400]{2,1,0:T(1,128)S(1)} all-to-all(f32[16,1,16400]{2,1,0:T(1,128)S(1)} %broadcast_in_dim.18), channel_id=1, replica_groups=mesh['row'=16,'col'=32] {'row'}, dimensions={0} | all-to-all | bytes 2099200 | tf_op jit(solution)/shard_map/all_to_all | solution.py:33
  301.2 48.2 %all-gather.2.cloned.1.call-done = f32[512,1025]{1,0:T(8,128)} async-done(((f32[16,1025]{1,0:T(8,128)}), f32[512,1025]{1,0:T(8,128)}) %all-gather.2.cloned.1.call-update) | async-done | bytes 2099216 | tf_op jit(solution)/shard_map/all_gather | solution.py:53
  349.5 2.4 slice_bitcast_fusion.1
  355.7 12.3 %cholesky.104 = f32[128,128]{1,0:T(8,128)} custom-call(f32[128,128]{1,0:T(8,128)S(1)} %cholesky.266), custom_call_target="Cholesky" | custom-call | tf_op jit(solution)/shard_map/jit(cholesky)/cholesky | solution.py:93
  370.4 11.3 %custom-call.32 = f32[1,128,128]{1,2,0:T(8,128)} custom-call(f32[1,128,128]{2,1,0:T(8,128)} %get-tuple-element.36), custom_call_target="InvertDiagBlocksLowerTriangular" | custom-call | tf_op jit(solution)/shard_map/jit(cholesky)/cholesky | solution.py:93
  385.5 13.2 %cholesky.217 = f32[128,128]{1,0:T(8,128)} custom-call(f32[128,128]{1,0:T(8,128)} %cholesky.270), custom_call_target="Cholesky" | custom-call | tf_op jit(solution)/shard_map/jit(cholesky)/cholesky | solution.py:93
  400.2 11.6 %custom-call.33 = f32[1,128,128]{1,2,0:T(8,128)} custom-call(f32[1,128,128]{2,1,0:T(8,128)} %get-tuple-element.33), custom_call_target="InvertDiagBlocksLowerTriangular" | custom-call | tf_op jit(solution)/shard_map/jit(cholesky)/cholesky | solution.py:93
  415.6 13.2 %cholesky.238 = f32[128,128]{1,0:T(8,128)} custom-call(f32[128,128]{1,0:T(8,128)} %cholesky.275), custom_call_target="Cholesky" | custom-call | tf_op jit(solution)/shard_map/jit(cholesky)/cholesky | solution.py:93
  430.9 11.3 %custom-call.34 = f32[1,128,128]{1,2,0:T(8,128)} custom-call(f32[1,128,128]{2,1,0:T(8,128)} %get-tuple-element.30), custom_call_target="InvertDiagBlocksLowerTriangular" | custom-call | tf_op jit(solution)/shard_map/jit(cholesky)/cholesky | solution.py:93
  445.1 13.3 %cholesky.255 = f32[128,128]{1,0:T(8,128)} custom-call(f32[128,128]{1,0:T(8,128)} %convolution_subtract_fusion.9), custom_call_target="Cholesky" | custom-call | tf_op jit(solution)/shard_map/jit(cholesky)/cholesky | solution.py:93
  464.3 14.2 %while.1 = (s32[]{:T(128)}, f32[512,512]{1,0:T(8,128)}, s32[4,2]{0,1:T(2,128)S(1)}, f32[4,128,128]{2,1,0:T(8,128)}, s32[]{:T(128)}) while((s32[]{:T(128)}, f32[512,512]{1,0:T(8,128)}, s32[4,2]{0,1:T(2,128)S(1)}, f32[4,128,128]{2,1,0:T(8,128)}, s32[]{:T(128)}) %tuple.50), condition=%wide.while_cond, body=%wide.while_body.sunk | while | flops 2 | bytes 132705 | solution.py:95
  464.9 2.9 bitcast_dynamic-update-slice_fusion.2
  468.5 2.9 bitcast_dynamic-update-slice_fusion.2
  472.1 2.9 bitcast_dynamic-update-slice_fusion.2
  475.6 2.8 bitcast_dynamic-update-slice_fusion.2
  478.5 40.7 %custom-call.35 = f32[4,128,128]{1,2,0:T(8,128)} custom-call(f32[4,128,128]{2,1,0:T(8,128)} %get-tuple-element.10), custom_call_target="InvertDiagBlocksLowerTriangular" | custom-call | tf_op jit(solution)/shard_map/triangular_solve | solution.py:95
  525.0 2.4 convolution_subtract_fusion.5
  532.3 2.3 convolution_subtract_fusion.4
  539.1 2.9 convolution_subtract_fusion.6
  (161 shorter events, 79.7 us)
Async XLA Ops:
  7.2 15.1 %copy-start = (f32[128,256]{1,0:T(8,128)S(1)}, f32[128,256]{1,0:T(8,128)}, u32[]{:S(2)}) copy-start(f32[128,256]{1,0:T(8,128)} %param.13) | copy-start | bytes 393220
  7.2 342.3 %all-gather.2.cloned.1.call-start = ((), (), s32[]{:S(2)}) async-start(), calls=%async_computation.2 | async-start | bytes 2433024 | tf_op jit(solution)/shard_map/all_gather | solution.py:53
  7.2 153.1 %collective-permute-start = (f32[3,128]{1,0:T(4,128)}, f32[3,128]{1,0:T(4,128)}, u32[]{:S(2)}, u32[]{:S(2)}) collective-permute-start(f32[3,128]{1,0:T(4,128)} %param.10), channel_id=1, source_target_pairs={{0,1},{1,2},{2,3},{3,4},{4,5},{5,6},{6,7},{7,8},{8,9},{9,10},{10,1... | collective-permute-start | bytes 4616 | tf_op jit(solution)/shard_map/ppermute | solution.py:64
  11.8 164.1 %collective-permute-start.2 = (f32[3,128]{1,0:T(4,128)}, f32[3,128]{1,0:T(4,128)}, u32[]{:S(2)}, u32[]{:S(2)}) collective-permute-start(f32[3,128]{1,0:T(4,128)} %param.10), channel_id=1, source_target_pairs={{1,0},{2,1},{3,2},{4,3},{5,4},{6,5},{7,6},{8,7},{9,8},{10,9},{11,1... | collective-permute-start | bytes 4616 | tf_op jit(solution)/shard_map/ppermute | solution.py:64
  17.9 158.8 %collective-permute-start.1 = (f32[128,512]{1,0:T(8,128)}, f32[128,512]{1,0:T(8,128)S(1)}, u32[]{:S(2)}, u32[]{:S(2)}) collective-permute-start(f32[128,512]{1,0:T(8,128)} %param.11), channel_id=1, source_target_pairs={{0,1},{1,2},{2,3},{3,4},{4,5},{5,6},{6,7},{7,8},{8,9},{9,10},{10,1... | collective-permute-start | bytes 786440 | tf_op jit(solution)/shard_map/ppermute | solution.py:64
  19.8 158.3 %collective-permute-start.3 = (f32[128,512]{1,0:T(8,128)}, f32[128,512]{1,0:T(8,128)S(1)}, u32[]{:S(2)}, u32[]{:S(2)}) collective-permute-start(f32[128,512]{1,0:T(8,128)} %param.11), channel_id=1, source_target_pairs={{1,0},{2,1},{3,2},{4,3},{5,4},{6,5},{7,6},{8,7},{9,8},{10,9},{11,1... | collective-permute-start | bytes 786440 | tf_op jit(solution)/shard_map/ppermute | solution.py:64
  23.8 29.7 %collective-permute-start.4 = (f32[256,512]{1,0:T(8,128)S(1)}, f32[256,512]{1,0:T(8,128)S(1)}, u32[]{:S(2)}, u32[]{:S(2)}) collective-permute-start(f32[256,512]{1,0:T(8,128)S(1)} %fusion.166), channel_id=1, source_target_pairs={{0,256},{256,0},{32,288},{288,32},{64,320},{320,64},{96,352},{352,... | collective-permute-start | bytes 1572872 | tf_op jit(solution)/shard_map/ppermute | solution.py:74
  56.2 79.0 %collective-permute-start.5 = (f32[256,512]{1,0:T(8,128)S(1)}, f32[256,512]{1,0:T(8,128)S(1)}, u32[]{:S(2)}, u32[]{:S(2)}) collective-permute-start(f32[256,512]{1,0:T(8,128)S(1)} %fusion), channel_id=1, source_target_pairs={{0,128},{128,0},{32,160},{160,32},{64,192},{192,64},{96,224},{224,... | collective-permute-start | bytes 1572872 | tf_op jit(solution)/shard_map/ppermute | solution.py:74
  136.1 4.3 copy-start.20
  136.2 4.3 copy-start.2
  137.9 16.4 %collective-permute-start.6 = (f32[256,512]{1,0:T(8,128)S(1)}, f32[256,512]{1,0:T(8,128)S(1)}, u32[]{:S(2)}, u32[]{:S(2)}) collective-permute-start(f32[256,512]{1,0:T(8,128)S(1)} %multiply_add_fusion.2), channel_id=1, source_target_pairs={{0,16},{16,0},{1,17},{17,1},{2,18},{18,2},{3,19},{19,3},{4,20},{20... | collective-permute-start | bytes 1572872 | tf_op jit(solution)/shard_map/ppermute | solution.py:74
  157.0 14.0 %collective-permute-start.7 = (f32[256,512]{1,0:T(8,128)S(1)}, f32[256,512]{1,0:T(8,128)S(1)}, u32[]{:S(2)}, u32[]{:S(2)}) collective-permute-start(f32[256,512]{1,0:T(8,128)S(1)} %multiply_add_fusion.1), channel_id=1, source_target_pairs={{0,8},{8,0},{1,9},{9,1},{2,10},{10,2},{3,11},{11,3},{4,12},{12,4},... | collective-permute-start | bytes 1572872 | tf_op jit(solution)/shard_map/ppermute | solution.py:74
  161.7 10.4 %copy-start.16 = (f32[1,256]{1,0:T(1,128)S(1)}, f32[1,256]{1,0:T(1,128)}, u32[]{:S(2)}) copy-start(f32[1,256]{1,0:T(1,128)} %get-tuple-element.39) | copy-start | bytes 3076
  172.1 4.6 copy-start.17
  172.1 4.6 copy-start.18
  172.1 4.6 copy-start.19
  173.8 14.6 %collective-permute-start.8 = (f32[256,512]{1,0:T(8,128)S(1)}, f32[256,512]{1,0:T(8,128)S(1)}, u32[]{:S(2)}, u32[]{:S(2)}) collective-permute-start(f32[256,512]{1,0:T(8,128)S(1)} %multiply_add_fusion), channel_id=1, source_target_pairs={{0,4},{4,0},{1,5},{5,1},{2,6},{6,2},{3,7},{7,3},{8,12},{12,8},{9,1... | collective-permute-start | bytes 1572872 | tf_op jit(solution)/shard_map/ppermute | solution.py:74
  179.4 10.1 %copy-start.21 = (pred[256]{0:T(512)(128)(4,1)S(1)}, pred[256]{0:T(512)(128)(4,1)}, u32[]{:S(2)}) copy-start(pred[256]{0:T(512)(128)(4,1)} %compare_and_fusion) | copy-start | bytes 772
  189.5 1.8 copy-start.14
  189.5 1.8 copy-start.15
  191.8 2.1 copy-start.5
  349.5 4.0 copy-start.1
  354.6 1.0 copy-start.7
  384.2 0.7 copy-start.12
  414.3 0.7 copy-start.13
  464.3 58.4 %copy-start.4 = (f32[512,512]{0,1:T(8,128)S(1)}, f32[512,512]{0,1:T(8,128)}, u32[]{:S(2)}) copy-start(f32[512,512]{0,1:T(8,128)} %get-tuple-element.22) | copy-start | bytes 3145732
  519.2 3.0 copy-start.9
  531.6 0.7 copy-start.8
  534.6 4.5 copy-start.3
  534.6 4.5 copy-start.6
  537.4 4.6 copy-start.10
  537.4 4.6 copy-start.11
Sparse Core Ops, SparseCore 0:
  301.4 48.0 all-gather.1
where the time goes:
time: 557 us; the launch traced here: 550 us
  other arithmetic  143 us (26%)
  waiting for transfers between devices  130 us (23%)
  blocking collectives  104 us (19%)
  starting transfers between devices  74.4 us (13%)
  matrix products  43 us (8%)
  local copies, waits for them, and re-layouts  38.3 us (7%)
  between operations  17.5 us (3%)
    another operation x14, other arithmetic, chol_solve(): factor = jnp.linalg.cholesky(gram_mat)  93.5 us
    ppermute x5, waiting for transfers between devices, from_partner(): return lax.ppermute(block, axis, route)  81.7 us
    all_to_all x1, blocking collectives, from_everyone(): lax.all_to_all(jnp.broadcast_to(shard[None], (length, *shard.shape)), axi...  66.4 us
    ppermute x5, starting transfers between devices, from_partner(): return lax.ppermute(block, axis, route)  59.3 us
    all_gather x1, waiting for transfers between devices, gather_turned(): lax.all_gather(both, axis, axis=0, tiled=True)  48.2 us
    another operation x3, other arithmetic, chol_solve(): lax.linalg.triangular_solve(factor, middle, left_side=True, lower=True, t...  41.9 us
    all_to_all x1, blocking collectives, sent_and_summed(): lax.all_to_all(in_blocks(shard, dim, length), axis, 0, 0, tiled=True)  37.4 us
    dot_general x10, matrix products, matmul_hi(): return jnp.dot(left, right, precision=lax.Precision.HIGHEST)  15.4 us
  transfers between devices with their start and end apart: 10, of which 6 were waited for; matrix products, arithmetic and copies ran while one was open for 5% of the time, Pallas kernels for 0%

commit v1 on v0

--- a/solution.py
+++ b/solution.py
@@ -7,6 +7,13 @@
 COL_LEVELS = 3
 WAVENUM = 6.0
 SOFTEN = 0.01
+
+
+def swapped_in(array, name, d):
+    peers = lax.axis_size(name)
+    blocks = jnp.stack([array for _ in range(peers)])
+    blocks = lax.all_to_all(blocks, name, split_axis=0, concat_axis=0)
+    return jnp.concatenate(blocks, axis=d)
 
 
 def in_blocks(shard, dim, length):
@@ -50,7 +57,7 @@
 def gather_turned(arrays, axis, dims):
     turned = [jnp.moveaxis(a, dim, 0) for a, dim in zip(arrays, dims)]
     both = jnp.concatenate([t.reshape(len(t), -1) for t in turned], axis=1)
-    whole, at, finished = (lax.all_gather(both, axis, axis=0, tiled=True), 0, [])
+    whole, at, finished = (swapped_in(both, axis, 0), 0, [])
     for t, dim in zip(turned, dims):
         piece = whole[:, at : at + t[0].size].reshape(-1, *t.shape[1:])
         finished.append(jnp.moveaxis(piece, 0, dim))

time: 557 us -> 533 us (0.957)
  waiting for transfers between devices: 130 us -> 112 us
  between operations: 17.5 us -> 4.08 us
    all_gather x1 -> x0, waiting for transfers between devices: 48.2 us -> none  [gather_turned(): lax.all_gather(both, axis, axis=0, tiled=True)]
    all_to_all x0 -> x1, waiting for transfers between devices: none -> 31 us  [swapped_in(): blocks = lax.all_to_all(blocks, name, split_axis=0, concat_axis=0)]
    another operation x12 -> x13, local copies, waits for them, and re-layouts: 14.2 us -> 15.6 us
where the time goes in v1:
time: 533 us; the launch traced here: 525 us
  other arithmetic  144 us (27%)
  waiting for transfers between devices  112 us (21%)
  blocking collectives  104 us (20%)
  starting transfers between devices  79.6 us (15%)
  matrix products  43.5 us (8%)
  local copies, waits for them, and re-layouts  39.1 us (7%)
    another operation x14, other arithmetic, chol_solve(): factor = jnp.linalg.cholesky(gram_mat)  93.6 us
    ppermute x5, waiting for transfers between devices, from_partner(): return lax.ppermute(block, axis, route)  80.9 us
    all_to_all x1, blocking collectives, from_everyone(): lax.all_to_all(jnp.broadcast_to(shard[None], (length, *shard.shape)), axi...  66.4 us
    ppermute x5, starting transfers between devices, from_partner(): return lax.ppermute(block, axis, route)  59.3 us
    another operation x3, other arithmetic, chol_solve(): lax.linalg.triangular_solve(factor, middle, left_side=True, lower=True, t...  41.9 us
    all_to_all x1, blocking collectives, sent_and_summed(): lax.all_to_all(in_blocks(shard, dim, length), axis, 0, 0, tiled=True)  37.4 us
    all_to_all x1, waiting for transfers between devices, swapped_in(): blocks = lax.all_to_all(blocks, name, split_axis=0, concat_axis=0)  31 us
    ppermute x4, starting transfers between devices, from_behind(): return lax.ppermute(block, axis, route)  15.1 us
  transfers between devices with their start and end apart: 10, of which 6 were waited for; matrix products, arithmetic and copies ran while one was open for 5% of the time, Pallas kernels for 0%

profile of v1, /device:TPU:1, one launch (start us, length us, event | category | flops | bytes accessed | tf_op | source)
XLA Modules:
  0.0 525.5 jit_solution(17205545126449687849)
XLA Ops:
  0.6 4.7 collective-permute-start
  5.4 6.1 %collective-permute-start.2 = (f32[3,128]{1,0:T(4,128)}, f32[3,128]{1,0:T(4,128)}, u32[]{:S(2)}, u32[]{:S(2)}) collective-permute-start(f32[3,128]{1,0:T(4,128)} %param.10), channel_id=1, source_target_pairs={{1,0},{2,1},{3,2},{4,3},{5,4},{6,5},{7,6},{8,7},{9,8},{10,9},{11,1... | collective-permute-start | bytes 4616 | tf_op jit(solution)/shard_map/ppermute | solution.py:71
  11.4 1.9 collective-permute-start.1
  13.4 2.4 collective-permute-start.3
  17.4 16.8 %collective-permute-start.4 = (f32[256,512]{1,0:T(8,128)S(1)}, f32[256,512]{1,0:T(8,128)S(1)}, u32[]{:S(2)}, u32[]{:S(2)}) collective-permute-start(f32[256,512]{1,0:T(8,128)S(1)} %fusion.166), channel_id=1, source_target_pairs={{0,256},{256,0},{32,288},{288,32},{64,320},{320,64},{96,352},{352,... | collective-permute-start | bytes 1572872 | tf_op jit(solution)/shard_map/ppermute | solution.py:81
  39.2 7.9 %collective-permute-done.4 = f32[256,512]{1,0:T(8,128)S(1)} collective-permute-done((f32[256,512]{1,0:T(8,128)S(1)}, f32[256,512]{1,0:T(8,128)S(1)}, u32[]{:S(2)}, u32[]{:S(2)}) %collective-permute-start.4) | collective-permute-done | bytes 524320 | tf_op jit(solution)/shard_map/ppermute | solution.py:81
  49.8 36.6 %collective-permute-start.5 = (f32[256,512]{1,0:T(8,128)S(1)}, f32[256,512]{1,0:T(8,128)S(1)}, u32[]{:S(2)}, u32[]{:S(2)}) collective-permute-start(f32[256,512]{1,0:T(8,128)S(1)} %fusion), channel_id=1, source_target_pairs={{0,128},{128,0},{32,160},{160,32},{64,192},{192,64},{96,224},{224,... | collective-permute-start | bytes 1572872 | tf_op jit(solution)/shard_map/ppermute | solution.py:81
  86.4 42.3 %collective-permute-done.5 = f32[256,512]{1,0:T(8,128)S(1)} collective-permute-done((f32[256,512]{1,0:T(8,128)S(1)}, f32[256,512]{1,0:T(8,128)S(1)}, u32[]{:S(2)}, u32[]{:S(2)}) %collective-permute-start.5) | collective-permute-done | bytes 524320 | tf_op jit(solution)/shard_map/ppermute | solution.py:81
  134.7 13.1 %collective-permute-done.6 = f32[256,512]{1,0:T(8,128)S(1)} collective-permute-done((f32[256,512]{1,0:T(8,128)S(1)}, f32[256,512]{1,0:T(8,128)S(1)}, u32[]{:S(2)}, u32[]{:S(2)}) %collective-permute-start.6) | collective-permute-done | bytes 524320 | tf_op jit(solution)/shard_map/ppermute | solution.py:81
  155.1 9.3 %collective-permute-done.7 = f32[256,512]{1,0:T(8,128)S(1)} collective-permute-done((f32[256,512]{1,0:T(8,128)S(1)}, f32[256,512]{1,0:T(8,128)S(1)}, u32[]{:S(2)}, u32[]{:S(2)}) %collective-permute-start.7) | collective-permute-done | bytes 524320 | tf_op jit(solution)/shard_map/ppermute | solution.py:81
  167.3 2.1 collective-permute-start.8
  170.2 2.0 fusion.4
  173.6 8.2 %collective-permute-done.8 = f32[256,512]{1,0:T(8,128)S(1)} collective-permute-done((f32[256,512]{1,0:T(8,128)S(1)}, f32[256,512]{1,0:T(8,128)S(1)}, u32[]{:S(2)}, u32[]{:S(2)}) %collective-permute-start.8) | collective-permute-done | bytes 524320 | tf_op jit(solution)/shard_map/ppermute | solution.py:81
  187.5 37.4 %all_to_all.16 = f32[32,1025,16]{1,2,0:T(8,128)S(1)} all-to-all(f32[32,1025,16]{1,2,0:T(8,128)S(1)} %maximum_bitcast_fusion), channel_id=1, replica_groups=mesh['row'=16,'col'=32] {'col'}, dimensions={0} | all-to-all | bytes 4198400 | tf_op jit(solution)/shard_map/all_to_all | solution.py:27
  226.3 66.4 %all_to_all.17 = f32[16,1,16400]{2,1,0:T(1,128)S(1)} all-to-all(f32[16,1,16400]{2,1,0:T(1,128)S(1)} %broadcast_in_dim.18), channel_id=1, replica_groups=mesh['row'=16,'col'=32] {'row'}, dimensions={0} | all-to-all | bytes 2099200 | tf_op jit(solution)/shard_map/all_to_all | solution.py:40
  295.5 5.1 all-to-all-start.2
  300.6 31.0 %all-to-all-done.2 = f32[32,16,1025]{2,1,0:T(8,128)S(1)} async-done(((f32[32,16,1025]{2,1,0:T(8,128)}), f32[32,16,1025]{2,1,0:T(8,128)S(1)}, u32[]{:S(2)}, u32[]{:S(2)}) %all-to-all-start.2) | async-done | bytes 2099232 | tf_op jit(solution)/shard_map/all_to_all | solution.py:15
  336.5 12.3 %cholesky.104 = f32[128,128]{1,0:T(8,128)} custom-call(f32[128,128]{1,0:T(8,128)S(1)} %cholesky.266), custom_call_target="Cholesky" | custom-call | tf_op jit(solution)/shard_map/jit(cholesky)/cholesky | solution.py:100
  351.3 11.3 %custom-call.32 = f32[1,128,128]{1,2,0:T(8,128)} custom-call(f32[1,128,128]{2,1,0:T(8,128)} %get-tuple-element.36), custom_call_target="InvertDiagBlocksLowerTriangular" | custom-call | tf_op jit(solution)/shard_map/jit(cholesky)/cholesky | solution.py:100
  366.4 13.2 %cholesky.217 = f32[128,128]{1,0:T(8,128)} custom-call(f32[128,128]{1,0:T(8,128)} %cholesky.270), custom_call_target="Cholesky" | custom-call | tf_op jit(solution)/shard_map/jit(cholesky)/cholesky | solution.py:100
  381.0 11.6 %custom-call.33 = f32[1,128,128]{1,2,0:T(8,128)} custom-call(f32[1,128,128]{2,1,0:T(8,128)} %get-tuple-element.33), custom_call_target="InvertDiagBlocksLowerTriangular" | custom-call | tf_op jit(solution)/shard_map/jit(cholesky)/cholesky | solution.py:100
  396.4 13.2 %cholesky.238 = f32[128,128]{1,0:T(8,128)} custom-call(f32[128,128]{1,0:T(8,128)} %cholesky.275), custom_call_target="Cholesky" | custom-call | tf_op jit(solution)/shard_map/jit(cholesky)/cholesky | solution.py:100
  411.8 11.3 %custom-call.34 = f32[1,128,128]{1,2,0:T(8,128)} custom-call(f32[1,128,128]{2,1,0:T(8,128)} %get-tuple-element.30), custom_call_target="InvertDiagBlocksLowerTriangular" | custom-call | tf_op jit(solution)/shard_map/jit(cholesky)/cholesky | solution.py:100
  426.0 13.2 %cholesky.255 = f32[128,128]{1,0:T(8,128)} custom-call(f32[128,128]{1,0:T(8,128)} %convolution_subtract_fusion.9), custom_call_target="Cholesky" | custom-call | tf_op jit(solution)/shard_map/jit(cholesky)/cholesky | solution.py:100
  445.2 14.0 %while.1 = (s32[]{:T(128)}, f32[512,512]{1,0:T(8,128)}, s32[4,2]{0,1:T(2,128)S(1)}, f32[4,128,128]{2,1,0:T(8,128)}, s32[]{:T(128)}) while((s32[]{:T(128)}, f32[512,512]{1,0:T(8,128)}, s32[4,2]{0,1:T(2,128)S(1)}, f32[4,128,128]{2,1,0:T(8,128)}, s32[]{:T(128)}) %tuple.50), condition=%wide.while_cond, body=%wide.while_body.sunk | while | flops 2 | bytes 132705 | solution.py:102
  445.9 2.9 bitcast_dynamic-update-slice_fusion.2
  449.4 2.9 bitcast_dynamic-update-slice_fusion.2
  452.9 2.9 bitcast_dynamic-update-slice_fusion.2
  456.5 2.8 bitcast_dynamic-update-slice_fusion.2
  459.2 40.7 %custom-call.35 = f32[4,128,128]{1,2,0:T(8,128)} custom-call(f32[4,128,128]{2,1,0:T(8,128)} %get-tuple-element.10), custom_call_target="InvertDiagBlocksLowerTriangular" | custom-call | tf_op jit(solution)/shard_map/triangular_solve | solution.py:102
  506.7 2.4 convolution_subtract_fusion.5
  513.9 2.3 convolution_subtract_fusion.4
  (155 shorter events, 85.2 us)
Async XLA Ops:
  0.6 15.2 %copy-start = (f32[128,256]{1,0:T(8,128)S(1)}, f32[128,256]{1,0:T(8,128)}, u32[]{:S(2)}) copy-start(f32[128,256]{1,0:T(8,128)} %param.13) | copy-start | bytes 393220
  0.6 153.1 %collective-permute-start = (f32[3,128]{1,0:T(4,128)}, f32[3,128]{1,0:T(4,128)}, u32[]{:S(2)}, u32[]{:S(2)}) collective-permute-start(f32[3,128]{1,0:T(4,128)} %param.10), channel_id=1, source_target_pairs={{0,1},{1,2},{2,3},{3,4},{4,5},{5,6},{6,7},{7,8},{8,9},{9,10},{10,1... | collective-permute-start | bytes 4616 | tf_op jit(solution)/shard_map/ppermute | solution.py:71
  5.4 164.0 %collective-permute-start.2 = (f32[3,128]{1,0:T(4,128)}, f32[3,128]{1,0:T(4,128)}, u32[]{:S(2)}, u32[]{:S(2)}) collective-permute-start(f32[3,128]{1,0:T(4,128)} %param.10), channel_id=1, source_target_pairs={{1,0},{2,1},{3,2},{4,3},{5,4},{6,5},{7,6},{8,7},{9,8},{10,9},{11,1... | collective-permute-start | bytes 4616 | tf_op jit(solution)/shard_map/ppermute | solution.py:71
  11.4 158.8 %collective-permute-start.1 = (f32[128,512]{1,0:T(8,128)}, f32[128,512]{1,0:T(8,128)S(1)}, u32[]{:S(2)}, u32[]{:S(2)}) collective-permute-start(f32[128,512]{1,0:T(8,128)} %param.11), channel_id=1, source_target_pairs={{0,1},{1,2},{2,3},{3,4},{4,5},{5,6},{6,7},{7,8},{8,9},{9,10},{10,1... | collective-permute-start | bytes 786440 | tf_op jit(solution)/shard_map/ppermute | solution.py:71
  13.4 158.8 %collective-permute-start.3 = (f32[128,512]{1,0:T(8,128)}, f32[128,512]{1,0:T(8,128)S(1)}, u32[]{:S(2)}, u32[]{:S(2)}) collective-permute-start(f32[128,512]{1,0:T(8,128)} %param.11), channel_id=1, source_target_pairs={{1,0},{2,1},{3,2},{4,3},{5,4},{6,5},{7,6},{8,7},{9,8},{10,9},{11,1... | collective-permute-start | bytes 786440 | tf_op jit(solution)/shard_map/ppermute | solution.py:71
  17.4 29.7 %collective-permute-start.4 = (f32[256,512]{1,0:T(8,128)S(1)}, f32[256,512]{1,0:T(8,128)S(1)}, u32[]{:S(2)}, u32[]{:S(2)}) collective-permute-start(f32[256,512]{1,0:T(8,128)S(1)} %fusion.166), channel_id=1, source_target_pairs={{0,256},{256,0},{32,288},{288,32},{64,320},{320,64},{96,352},{352,... | collective-permute-start | bytes 1572872 | tf_op jit(solution)/shard_map/ppermute | solution.py:81
  49.8 79.0 %collective-permute-start.5 = (f32[256,512]{1,0:T(8,128)S(1)}, f32[256,512]{1,0:T(8,128)S(1)}, u32[]{:S(2)}, u32[]{:S(2)}) collective-permute-start(f32[256,512]{1,0:T(8,128)S(1)} %fusion), channel_id=1, source_target_pairs={{0,128},{128,0},{32,160},{160,32},{64,192},{192,64},{96,224},{224,... | collective-permute-start | bytes 1572872 | tf_op jit(solution)/shard_map/ppermute | solution.py:81
  86.4 47.5 %copy-start.17 = (f32[3,128]{1,0:T(4,128)S(1)}, f32[3,128]{1,0:T(4,128)}, u32[]{:S(2)}) copy-start(f32[3,128]{1,0:T(4,128)} %param.10) | copy-start | bytes 4612
  86.4 47.5 %copy-start.1 = (f32[128,512]{1,0:T(8,128)S(1)}, f32[128,512]{1,0:T(8,128)}, u32[]{:S(2)}) copy-start(f32[128,512]{1,0:T(8,128)} %param.11) | copy-start | bytes 786436
  131.4 16.4 %collective-permute-start.6 = (f32[256,512]{1,0:T(8,128)S(1)}, f32[256,512]{1,0:T(8,128)S(1)}, u32[]{:S(2)}, u32[]{:S(2)}) collective-permute-start(f32[256,512]{1,0:T(8,128)S(1)} %multiply_add_fusion.2), channel_id=1, source_target_pairs={{0,16},{16,0},{1,17},{17,1},{2,18},{18,2},{3,19},{19,3},{4,20},{20... | collective-permute-start | bytes 1572872 | tf_op jit(solution)/shard_map/ppermute | solution.py:81
  150.5 14.0 %collective-permute-start.7 = (f32[256,512]{1,0:T(8,128)S(1)}, f32[256,512]{1,0:T(8,128)S(1)}, u32[]{:S(2)}, u32[]{:S(2)}) collective-permute-start(f32[256,512]{1,0:T(8,128)S(1)} %multiply_add_fusion.1), channel_id=1, source_target_pairs={{0,8},{8,0},{1,9},{9,1},{2,10},{10,2},{3,11},{11,3},{4,12},{12,4},... | collective-permute-start | bytes 1572872 | tf_op jit(solution)/shard_map/ppermute | solution.py:81
  155.1 10.4 %copy-start.16 = (f32[1,256]{1,0:T(1,128)S(1)}, f32[1,256]{1,0:T(1,128)}, u32[]{:S(2)}) copy-start(f32[1,256]{1,0:T(1,128)} %get-tuple-element.39) | copy-start | bytes 3076
  167.3 14.6 %collective-permute-start.8 = (f32[256,512]{1,0:T(8,128)S(1)}, f32[256,512]{1,0:T(8,128)S(1)}, u32[]{:S(2)}, u32[]{:S(2)}) collective-permute-start(f32[256,512]{1,0:T(8,128)S(1)} %multiply_add_fusion), channel_id=1, source_target_pairs={{0,4},{4,0},{1,5},{5,1},{2,6},{6,2},{3,7},{7,3},{8,12},{12,8},{9,1... | collective-permute-start | bytes 1572872 | tf_op jit(solution)/shard_map/ppermute | solution.py:81
  173.6 9.4 %copy-start.18 = (pred[256]{0:T(512)(128)(4,1)S(1)}, pred[256]{0:T(512)(128)(4,1)}, u32[]{:S(2)}) copy-start(pred[256]{0:T(512)(128)(4,1)} %compare_and_fusion) | copy-start | bytes 772
  173.6 11.1 %copy-start.14 = (f32[128,256]{1,0:T(8,128)S(1)}, f32[128,256]{1,0:T(8,128)}, u32[]{:S(2)}) copy-start(f32[128,256]{1,0:T(8,128)} %param.14) | copy-start | bytes 393220
  173.6 11.1 %copy-start.15 = (f32[1,256]{1,0:T(1,128)S(1)}, f32[1,256]{1,0:T(1,128)}, u32[]{:S(2)}) copy-start(f32[1,256]{1,0:T(1,128)} %get-tuple-element.37) | copy-start | bytes 3076
  185.2 2.1 copy-start.4
  295.5 36.1 %all-to-all-start.2 = ((f32[32,16,1025]{2,1,0:T(8,128)}), f32[32,16,1025]{2,1,0:T(8,128)S(1)}, u32[]{:S(2)}, u32[]{:S(2)}) async-start(f32[32,16,1025]{2,1,0:T(8,128)} %stack.2), calls=%async_computation.2 | async-start | bytes 4718592 | tf_op jit(solution)/shard_map/all_to_all | solution.py:15
  335.4 1.0 copy-start.6
  365.1 0.7 copy-start.12
  395.1 0.7 copy-start.13
  445.2 59.1 %copy-start.3 = (f32[512,512]{0,1:T(8,128)S(1)}, f32[512,512]{0,1:T(8,128)}, u32[]{:S(2)}) copy-start(f32[512,512]{0,1:T(8,128)} %get-tuple-element.22) | copy-start | bytes 3145732
  500.0 6.2 %copy-start.8 = (f32[4,128,128]{1,2,0:T(8,128)S(1)}, f32[4,128,128]{1,2,0:T(8,128)}, u32[]{:S(2)}) copy-start(f32[4,128,128]{1,2,0:T(8,128)} %custom-call.35) | copy-start | bytes 786436
  513.2 0.7 copy-start.7
  516.2 6.6 %copy-start.2 = (f32[128,512]{1,0:T(8,128)S(1)}, f32[128,512]{1,0:T(8,128)}, u32[]{:S(2)}) copy-start(f32[128,512]{1,0:T(8,128)} %param.11) | copy-start | bytes 786436
  516.2 6.6 %copy-start.5 = (f32[128,512]{1,0:T(8,128)S(1)}, f32[128,512]{1,0:T(8,128)}, u32[]{:S(2)}) copy-start(f32[128,512]{1,0:T(8,128)} %copy-done.4) | copy-start | bytes 786436
  518.9 3.9 copy-start.9
  519.7 3.1 copy-start.10
  519.7 3.1 copy-start.11
